TPU v7x, 32 devices: a whole 2x2x4 slice. The times are simulated.
32 devices in a mesh: dp: 4 (over z), expert: 8 (over y, x, core).
Axes of the slice: x: 2, y: 2, z: 4, core: 2. Of those that a mesh axis runs over, the one named last changes fastest.
Arguments:
- x_routed: bfloat16 [8, 512, 2048], P(None, 'dp', 'expert'), may hold values from -10 to 10
- grad_out: bfloat16 [8, 512, 768], P(None, 'dp'), may hold values from -15 to 15
- block_counts: int32 [4, 8], P('dp'), may hold values from 1 to 8, as said below
Outputs:
- update: bfloat16 [8, 2048, 768], P(None, 'expert')
Inputs may be any that keep to these rules, and one draw needn't show every extreme that they name: Rows of replica r beyond 16 * block_counts[r, e] of expert e are padding; on every replica one expert has all 128 rows live.
All inputs are finite; a program needn't handle non-finite values.
Results may differ from a plain program's by a relative error of at most 0.0065.
Values may be sent and summed in bfloat16 or wider, within the bound.
A program may use at most 64 MiB of HBM per device.

v0:
```python
import math

import jax
import jax.numpy as jnp
from jax import lax
from jax.sharding import PartitionSpec as P

D = 2048
BLK = 16
ITERS = 2


NEWTON_FIRST = 3.4445
NEWTON_SECOND = -4.775
NEWTON_THIRD = 2.0315
EPSILON = 1e-07


def masked_rows(grad_out, block_counts):
    capacity = grad_out.shape[1]
    row_index = lax.broadcasted_iota(jnp.int32, (grad_out.shape[0], capacity), 1)
    live_mask = row_index < BLK * block_counts[0][:, None]
    return jnp.where(live_mask[:, :, None], grad_out, jnp.zeros((), grad_out.dtype))


def newton_turn(current, gram_matrix, final_turn):
    square = jnp.dot(gram_matrix, gram_matrix, preferred_element_type=jnp.float32)
    polynomial = (NEWTON_SECOND * gram_matrix.astype(jnp.float32) + NEWTON_THIRD * square).astype(
        jnp.bfloat16
    )
    combined = NEWTON_FIRST * current.astype(jnp.float32) + jnp.dot(
        current, polynomial, preferred_element_type=jnp.float32
    )
    if final_turn:
        combined = combined * math.sqrt(D)
    return combined.astype(jnp.bfloat16)


def local_gram(current):
    return lax.dot_general(
        current, current, (((0,), (0,)), ((), ())), preferred_element_type=jnp.float32
    )


def per_device(x_routed, grad_out, block_counts):
    slice_width = x_routed.shape[2]
    hidden_width = grad_out.shape[2]
    groups = lax.axis_size("expert")
    replicas = lax.axis_size("dp")
    row_share = slice_width // replicas
    masked = masked_rows(grad_out, block_counts)
    partial_value = jnp.einsum("enk,enf->ekf", x_routed, masked, preferred_element_type=jnp.float32)
    gathered = lax.all_to_all(partial_value, "expert", split_axis=0, concat_axis=1, tiled=True)
    blocked = gathered.reshape(groups, replicas, row_share, hidden_width)
    owned = lax.psum_scatter(blocked, "dp", scatter_dimension=1, tiled=True).reshape(
        groups * row_share, hidden_width
    )
    norm_total = lax.psum(jnp.sum(owned * owned), "dp")
    current = (owned / (jnp.sqrt(norm_total) + EPSILON)).astype(jnp.bfloat16)
    gathered_rows = lax.all_gather(current, "dp", axis=0, tiled=True)
    for iteration in range(ITERS):
        gram_matrix = local_gram(gathered_rows).astype(jnp.bfloat16)
        gathered_rows = newton_turn(gathered_rows, gram_matrix, iteration + 1 == ITERS)
    arranged = gathered_rows.reshape(replicas, groups, row_share, hidden_width)
    returned = lax.all_to_all(arranged, "expert", split_axis=1, concat_axis=0, tiled=True)
    return returned.reshape(groups, replicas * row_share, hidden_width)


def solution(mesh):
    return jax.shard_map(
        per_device,
        mesh=mesh,
        in_specs=(P(None, "dp", "expert"), P(None, "dp", None), P("dp", None)),
        out_specs=P(None, "expert", None),
        check_vma=False,
    )
```

profile of v0, /device:TPU:1, one launch (start us, length us, event | category | flops | bytes accessed | tf_op | source)
XLA Modules:
  0.0 472.9 jit_solution(14418735263828322840)
XLA Ops:
  6.5 0.0 copy-start
  6.5 0.7 multiply_bitcast_fusion
  7.3 0.1 iota_compare_fusion
  7.3 0.3 copy-done
  7.6 2.5 convolution_bitcast_fusion
  10.1 75.3 %all_to_all.24 = f32[8,256,768]{1,2,0:T(8,128)} all-to-all(f32[8,256,768]{1,2,0:T(8,128)S(1)} %convolution_bitcast_fusion), channel_id=1, replica_groups=mesh['dp'=4,'expert'=8] {'expert'}, dimensions={0} | all-to-all | bytes 12582912 | tf_op jit(solution)/shard_map/all_to_all | solution.py:53
  85.5 6.6 %copy.11 = f32[8,256,768]{2,1,0:T(8,128)} copy(f32[8,256,768]{1,2,0:T(8,128)} %all_to_all.24) | data formatting | bytes 12582912 | tf_op jit(solution)/shard_map/all_to_all | solution.py:53
  92.1 0.0 all-reduce.3.cloned.1.call-update
  92.1 0.0 all-gather.2.cloned.1.call-start
  92.2 0.6 copy-done.1
  92.7 0.6 dynamic-slice
  93.4 221.8 %all-reduce.3.cloned.1.call-done = f32[8,4,64,768]{3,2,1,0:T(8,128)} async-done(((f32[8,4,64,768]{3,2,1,0:T(8,128)}), f32[8,4,64,768]{3,2,1,0:T(8,128)}) %all-reduce.3.cloned.1.call-update) | async-done | bytes 6291472
  315.1 3.0 multiply_reduce_fusion
  318.2 8.2 %psum.7 = f32[]{:T(128)} all-reduce(f32[]{:T(128)} %multiply_reduce_fusion), channel_id=1, replica_groups=mesh['dp'=4,'expert'=8] {'dp'}, use_global_device_ids=true, to_apply=%region_2.3 | all-reduce | flops 1 | bytes 8 | tf_op jit(solution)/shard_map/psum | solution.py:58
  327.0 3.0 divide_convert_fusion
  330.1 0.0 all-gather.2.cloned.1.call-update
  330.1 64.0 %all-gather.2.cloned.1.call-done = bf16[2048,768]{1,0:T(8,128)(2,1)} async-done(((bf16[512,768]{1,0:T(8,128)(2,1)}), bf16[2048,768]{1,0:T(8,128)(2,1)}) %all-gather.2.cloned.1.call-update) | async-done | bytes 3145744 | tf_op jit(solution)/shard_map/all_gather | solution.py:60
  394.1 5.5 %convolution_convert_fusion.1 = bf16[768,768]{1,0:T(8,128)(2,1)S(1)} fusion(bf16[2048,768]{1,0:T(8,128)(2,1)} %all-gather.2.cloned.1.call-done), kind=kOutput, calls=%fused_computation.10 | convolution fusion | flops 2416508928 | bytes 4325376 | tf_op jit(solution)/shard_map/dot_general | solution.py:40
  399.6 8.1 %add_convert_fusion = bf16[2048,768]{1,0:T(8,128)(2,1)} fusion(bf16[2048,768]{1,0:T(8,128)(2,1)} %all-gather.2.cloned.1.call-done, bf16[768,768]{1,0:T(8,128)(2,1)S(1)} %convolution_convert_fusion.1), kind=kOutput, calls=%fused_computation.1 | convolution fusion | flops 3331129344 | bytes 7471104 | tf_op jit(solution)/shard_map/dot_general | solution.py:31
  407.7 5.5 %convolution_convert_fusion = bf16[768,768]{1,0:T(8,128)(2,1)S(1)} fusion(bf16[2048,768]{1,0:T(8,128)(2,1)} %add_convert_fusion), kind=kOutput, calls=%fused_computation.9 | convolution fusion | flops 2416508928 | bytes 4325376 | tf_op jit(solution)/shard_map/dot_general | solution.py:40
  413.2 8.3 %multiply_convert_fusion = bf16[2048,768]{1,0:T(8,128)(2,1)} fusion(bf16[2048,768]{1,0:T(8,128)(2,1)} %add_convert_fusion, bf16[768,768]{1,0:T(8,128)(2,1)S(1)} %convolution_convert_fusion), kind=kOutput, calls=%fused_computation | convolution fusion | flops 3332702208 | bytes 7471104 | tf_op jit(solution)/shard_map/dot_general | solution.py:31
  421.5 2.2 copy.12
  423.7 40.7 %all_to_all.25 = bf16[4,8,64,768]{3,2,0,1:T(8,128)(2,1)S(1)} all-to-all(bf16[4,8,64,768]{3,2,0,1:T(8,128)(2,1)S(1)} %copy.12), channel_id=1, replica_groups=mesh['dp'=4,'expert'=8] {'expert'}, dimensions={1} | all-to-all | bytes 6291456 | tf_op jit(solution)/shard_map/all_to_all | solution.py:65
  464.4 1.7 copy.18
  (2 shorter events, 0.0 us)
Async XLA Ops:
  6.5 1.1 copy-start
  6.5 308.6 %all-reduce.3.cloned.1.call-start = ((), (), s32[]{:S(2)}) async-start(), calls=%async_computation.3 | async-start | bytes 12582912
  92.1 0.7 copy-start.1
  92.1 302.0 %all-gather.2.cloned.1.call-start = ((), (), s32[]{:S(2)}) async-start(), calls=%async_computation.2 | async-start | bytes 3932160 | tf_op jit(solution)/shard_map/all_gather | solution.py:60
Sparse Core Ops, SparseCore 0:
  92.2 222.8 all-reduce.2
  330.2 63.8 all-gather.1
where the time goes:
time: 475 us; the launch traced here: 473 us
  waiting for transfers between devices  286 us (60%)
  blocking collectives  124 us (26%)
  matrix products  29.9 us (6%)
  between operations  14.1 us (3%)
  local copies, waits for them, and re-layouts  11.9 us (3%)
  other arithmetic  6.83 us (1%)
    unnamed x3, waiting for transfers between devices  222 us
    all_to_all x1, blocking collectives, per_device(): lax.all_to_all(partial_value, 'expert', split_axis=0, concat_axis=1, tile...  75.3 us
    all_gather x1, waiting for transfers between devices, per_device(): gathered_rows = lax.all_gather(current, 'dp', axis=0, tiled=True)  64 us
    all_to_all x1, blocking collectives, per_device(): lax.all_to_all(arranged, 'expert', split_axis=1, concat_axis=0, tiled=True)  40.7 us
    dot_general x2, matrix products, newton_turn(): jnp.dot(current, polynomial, preferred_element_type=jnp.float32)  16.4 us
    dot_general x2, matrix products, local_gram(): lax.dot_general(current, current, (((0,), (0,)), ((), ())), preferred_ele...  11 us
  transfers between devices with their start and end apart: 2, of which 2 were waited for; matrix products, arithmetic and copies ran while one was open for 0% of the time, Pallas kernels for 0%

commit v1 on v0

v1 whole, which is shorter than its diff:
```python
import math

import jax
import jax.numpy as jnp
from jax import lax
from jax.sharding import PartitionSpec as P

D = 2048
BLK = 16
ITERS = 2


NEWTON_FIRST = 3.4445
NEWTON_SECOND = -4.775
NEWTON_THIRD = 2.0315
EPSILON = 1e-07


def newton_turn(current, gram_matrix, final_turn):
    square = jnp.dot(gram_matrix, gram_matrix, preferred_element_type=jnp.float32)
    polynomial = (NEWTON_SECOND * gram_matrix.astype(jnp.float32) + NEWTON_THIRD * square).astype(
        jnp.bfloat16
    )
    combined = NEWTON_FIRST * current.astype(jnp.float32) + jnp.dot(
        current, polynomial, preferred_element_type=jnp.float32
    )
    if final_turn:
        combined = combined * math.sqrt(D)
    return combined.astype(jnp.bfloat16)


def contract_rows(left, right):
    return lax.dot_general(
        left, right, (((0,), (0,)), ((), ())), preferred_element_type=jnp.float32
    )


def per_device(x_routed, grad_out, block_counts):
    slice_width = x_routed.shape[2]
    capacity, hidden_width = grad_out.shape[1:]
    groups = lax.axis_size("expert")
    expert = lax.axis_index("expert")
    x_rows = lax.all_to_all(x_routed, "expert", split_axis=0, concat_axis=2, tiled=True)[0]
    g_rows = lax.dynamic_index_in_dim(grad_out, expert, 0, keepdims=False)
    count = lax.dynamic_index_in_dim(block_counts[0], expert, 0, keepdims=False)
    row_index = lax.broadcasted_iota(jnp.int32, (capacity, 1), 0)
    g_rows = jnp.where(row_index < BLK * count, g_rows, jnp.zeros((), g_rows.dtype))
    g_all = lax.all_gather(g_rows, "dp", axis=0, tiled=True)
    x_all = lax.all_gather(x_rows, "dp", axis=0, tiled=True)
    gradient = contract_rows(x_all, g_all)
    norm_total = jnp.sum(gradient * gradient)
    current = (gradient / (jnp.sqrt(norm_total) + EPSILON)).astype(jnp.bfloat16)
    for iteration in range(ITERS):
        gram_matrix = contract_rows(current, current).astype(jnp.bfloat16)
        current = newton_turn(current, gram_matrix, iteration + 1 == ITERS)
    arranged = current.reshape(groups, slice_width, hidden_width)
    return lax.all_to_all(arranged, "expert", split_axis=0, concat_axis=0, tiled=True)


def solution(mesh):
    return jax.shard_map(
        per_device,
        mesh=mesh,
        in_specs=(P(None, "dp", "expert"), P(None, "dp", None), P("dp", None)),
        out_specs=P(None, "expert", None),
        check_vma=False,
    )
```

time: 475 us -> 170 us (0.36)
  waiting for transfers between devices: 286 us -> 26.6 us
  blocking collectives: 124 us -> 78.8 us
  matrix products: 29.9 us -> 39.7 us
  local copies, waits for them, and re-layouts: 11.9 us -> 6.15 us
    unnamed x3 -> x1, waiting for transfers between devices: 222 us -> 0.02 us
    all_to_all x2, blocking collectives: 116 us -> 53 us  [the longest x1 39.5 us: per_device(): lax.all_to_all(arranged, 'expert', split_axis=0, concat_axis=0, tiled=True)]
    all_gather x1, waiting for transfers between devices: 64 us -> 26.5 us  [per_device(): x_all = lax.all_gather(x_rows, 'dp', axis=0, tiled=True)]
    all_gather x0 -> x1, blocking collectives: none -> 25.8 us  [per_device(): g_all = lax.all_gather(g_rows, 'dp', axis=0, tiled=True)]
    psum x1 -> x0, blocking collectives: 8.18 us -> none  [per_device(): norm_total = lax.psum(jnp.sum(owned * owned), 'dp')]
    all_to_all x1 -> x0, local copies, waits for them, and re-layouts: 6.6 us -> none  [per_device(): lax.all_to_all(partial_value, 'expert', split_axis=0, concat_axis=1, tile...]
    dot_general x3, matrix products: 13.6 us -> 18.7 us  [contract_rows(): lax.dot_general(left, right, (((0,), (0,)), ((), ())), preferred_element_...]
  transfers between devices with their start and end apart: 2 -> 1, of which waited for: 2 -> 1; matrix products, arithmetic and copies ran while one was open for 0% -> 2% of each run, Pallas kernels for 0% -> 0%
where the time goes in v1:
time: 170 us; the launch traced here: 168 us
  blocking collectives  78.8 us (46%)
  matrix products  39.7 us (23%)
  waiting for transfers between devices  26.6 us (16%)
  between operations  14.1 us (8%)
  local copies, waits for them, and re-layouts  6.15 us (4%)
  other arithmetic  2.91 us (2%)
    all_to_all x1, blocking collectives, per_device(): lax.all_to_all(arranged, 'expert', split_axis=0, concat_axis=0, tiled=True)  39.5 us
    all_gather x1, waiting for transfers between devices, per_device(): x_all = lax.all_gather(x_rows, 'dp', axis=0, tiled=True)  26.5 us
    all_gather x1, blocking collectives, per_device(): g_all = lax.all_gather(g_rows, 'dp', axis=0, tiled=True)  25.8 us
    dot_general x2, matrix products, newton_turn(): jnp.dot(current, polynomial, preferred_element_type=jnp.float32)  21 us
    dot_general x3, matrix products, contract_rows(): lax.dot_general(left, right, (((0,), (0,)), ((), ())), preferred_element_...  18.7 us
    all_to_all x1, blocking collectives, per_device(): lax.all_to_all(x_routed, 'expert', split_axis=0, concat_axis=2, tiled=True)  13.5 us
  transfers between devices with their start and end apart: 1, of which 1 were waited for; matrix products, arithmetic and copies ran while one was open for 2% of the time, Pallas kernels for 0%

profile of v1, /device:TPU:1, one launch (start us, length us, event | category | flops | bytes accessed | tf_op | source)
XLA Modules:
  0.0 168.3 jit_solution(7677205352609327847)
XLA Ops:
  6.5 0.0 all-gather.2.cloned.1.call-start
  6.5 1.3 copy.7
  7.9 13.5 %all_to_all.20 = bf16[8,128,256]{1,2,0:T(8,128)(2,1)} all-to-all(bf16[8,128,256]{1,2,0:T(8,128)(2,1)S(1)} %copy.7), channel_id=1, replica_groups=mesh['dp'=4,'expert'=8] {'expert'}, dimensions={0} | all-to-all | bytes 1048576 | tf_op jit(solution)/shard_map/all_to_all | solution.py:43
  21.4 0.0 all-gather.2.cloned.1.call-update
  21.4 1.2 fusion.5
  22.7 0.6 iota_compare_fusion
  23.3 1.0 bitcast_select_fusion
  24.4 25.8 %all_gather.6 = bf16[512,768]{1,0:T(8,128)(2,1)S(1)} all-gather(bf16[128,768]{1,0:T(8,128)(2,1)S(1)} %bitcast_select_fusion), channel_id=1, replica_groups=mesh['dp'=4,'expert'=8] {'dp'}, dimensions={0}, use_global_device_ids=true | all-gather | bytes 983040 | tf_op jit(solution)/shard_map/all_gather | solution.py:48
  50.1 26.5 %all-gather.2.cloned.1.call-done = bf16[512,2048]{0,1:T(8,128)(2,1)} async-done(((bf16[128,2048]{0,1:T(8,128)(2,1)}), bf16[512,2048]{0,1:T(8,128)(2,1)}) %all-gather.2.cloned.1.call-update) | async-done | bytes 2097168 | tf_op jit(solution)/shard_map/all_gather | solution.py:49
  76.7 6.8 %multiply_reduce_fusion = (f32[]{:T(128)}, f32[768,2048]{1,0:T(8,128)}) fusion(bf16[512,768]{1,0:T(8,128)(2,1)S(1)} %all_gather.6, bf16[512,2048]{0,1:T(8,128)(2,1)} %all-gather.2.cloned.1.call-done), kind=kOutput, calls=%fused_computation.4 | convolution fusion | flops 1613758464 | bytes 9175044 | tf_op jit(solution)/shard_map/dot_general | solution.py:33
  84.1 8.3 %convolution_convert_fusion.1 = bf16[768,768]{1,0:T(8,128)(2,1)} fusion(f32[768,2048]{1,0:T(8,128)} %get-tuple-element.6, f32[]{:T(128)S(6)} %add.22), kind=kOutput, calls=%fused_computation.8 | convolution fusion | flops 2419654656 | bytes 7471108 | tf_op jit(solution)/shard_map/dot_general | solution.py:33
  92.4 12.6 %fusion = bf16[2048,768]{0,1:T(8,128)(2,1)S(1)} fusion(bf16[768,768]{1,0:T(8,128)(2,1)} %convolution_convert_fusion.1, f32[768,2048]{1,0:T(8,128)} %get-tuple-element.6, f32[]{:T(128)S(6)} %add.22), kind=kOutput, calls=%fused_computation.1 | convolution fusion | flops 3337420800 | bytes 10616836 | tf_op jit(solution)/shard_map/dot_general | solution.py:24
  105.0 3.6 %convolution_convert_fusion = bf16[768,768]{1,0:T(8,128)(2,1)} fusion(bf16[2048,768]{0,1:T(8,128)(2,1)S(1)} %fusion), kind=kOutput, calls=%fused_computation.7 | convolution fusion | flops 2416508928 | bytes 4325376 | tf_op jit(solution)/shard_map/dot_general | solution.py:33
  108.7 8.4 %multiply_convert_fusion = bf16[2048,768]{0,1:T(8,128)(2,1)} fusion(bf16[2048,768]{0,1:T(8,128)(2,1)S(1)} %fusion, bf16[768,768]{1,0:T(8,128)(2,1)} %convolution_convert_fusion), kind=kOutput, calls=%fused_computation.2 | convolution fusion | flops 3332702208 | bytes 7471104 | tf_op jit(solution)/shard_map/dot_general | solution.py:24
  117.1 3.2 %copy.13 = bf16[2048,768]{1,0:T(8,128)(2,1)S(1)} copy(bf16[2048,768]{0,1:T(8,128)(2,1)} %multiply_convert_fusion) | data formatting | bytes 6291456 | tf_op jit(solution)/shard_map/reshape | solution.py:56
  120.3 39.5 %all_to_all.21 = bf16[8,256,768]{2,1,0:T(8,128)(2,1)S(1)} all-to-all(bf16[8,256,768]{2,1,0:T(8,128)(2,1)S(1)} %bitcast.22), channel_id=1, replica_groups=mesh['dp'=4,'expert'=8] {'expert'}, dimensions={0} | all-to-all | bytes 6291456 | tf_op jit(solution)/shard_map/all_to_all | solution.py:57
  159.8 1.7 copy.15
Async XLA Ops:
  6.5 70.2 %all-gather.2.cloned.1.call-start = ((), (), s32[]{:S(2)}) async-start(), calls=%async_computation.2 | async-start | bytes 2621440 | tf_op jit(solution)/shard_map/all_gather | solution.py:49
Sparse Core Ops, SparseCore 0:
  21.5 55.0 all-gather.1

commit v2 on v1

v2 whole, which is shorter than its diff:
```python
import functools
import math

import jax
import jax.numpy as jnp
from jax import lax
from jax.experimental import pallas as pl
from jax.experimental.pallas import tpu as pltpu
from jax.sharding import PartitionSpec as P

D = 2048
BLK = 16
ITERS = 2


NEWTON_FIRST = 3.4445
NEWTON_SECOND = -4.775
NEWTON_THIRD = 2.0315
EPSILON = 1e-07
TILE = 256
MESH = pl.DeviceIdType.MESH


def contract_rows(left, right):
    return lax.dot_general(
        left, right, (((0,), (0,)), ((), ())), preferred_element_type=jnp.float32
    )


def gram_into(gram_ref, rows_ref, scale):
    groups, width, hidden = rows_ref.shape
    for low in range(0, hidden, TILE):
        left = rows_ref[:, :, low : low + TILE].reshape(groups * width, TILE)
        right = rows_ref[:, :, low:].reshape(groups * width, hidden - low)
        strip = contract_rows(left, right)
        if scale is not None:
            strip = strip * scale
        gram_ref[low : low + TILE, low:] = strip.astype(jnp.bfloat16)
        for other in range(low + TILE, hidden, TILE):
            block = strip[:, other - low : other - low + TILE]
            gram_ref[other : other + TILE, low : low + TILE] = block.T.astype(jnp.bfloat16)


def polynomial_into(poly_ref, gram_ref):
    hidden = gram_ref.shape[0]
    for low in range(0, hidden, TILE):
        strip = gram_ref[low : low + TILE, :]
        square = jnp.dot(strip, gram_ref[...], preferred_element_type=jnp.float32)
        poly_ref[low : low + TILE, :] = (
            NEWTON_SECOND * strip.astype(jnp.float32) + NEWTON_THIRD * square
        ).astype(jnp.bfloat16)


def turn(rows, poly_ref):
    return NEWTON_FIRST * rows.astype(jnp.float32) + jnp.dot(
        rows, poly_ref[...], preferred_element_type=jnp.float32
    )


def kernel(
    groups,
    replicas,
    parts,
    counts_ref,
    x_ref,
    g_ref,
    out_ref,
    x_all,
    g_all,
    g_raw,
    grad,
    current,
    stage,
    gram,
    poly,
    local_sem,
    x_send,
    x_recv,
    right_send,
    left_send,
    line_recv,
    out_send,
    out_recv,
):
    z = lax.axis_index("dp")
    me = lax.axis_index("expert")
    capacity = g_raw.shape[0]
    per_part = groups // parts
    last = replicas - 1
    right_exists = z < last
    left_exists = z > 0

    barrier = pltpu.get_barrier_semaphore()

    def greet(step, carry):
        peer = lax.rem(me + step, groups)
        pl.semaphore_signal(barrier, inc=1, device_id=(z, peer), device_id_type=MESH)
        return carry

    lax.fori_loop(1, groups, greet, 0)

    @pl.when(right_exists)
    def _():
        pl.semaphore_signal(barrier, inc=1, device_id=(z + 1, me), device_id_type=MESH)

    @pl.when(left_exists)
    def _():
        pl.semaphore_signal(barrier, inc=1, device_id=(z - 1, me), device_id_type=MESH)

    own_g = pltpu.make_async_copy(g_ref.at[me], g_raw, local_sem.at[0])
    own_g.start()
    own_x = pltpu.make_async_copy(x_ref.at[me], x_all.at[z, me], local_sem.at[1])
    own_x.start()

    neighbours = jnp.minimum(z, 1) + jnp.minimum(last - z, 1)
    pl.semaphore_wait(barrier, groups - 1 + neighbours)

    def x_copy(peer):
        return pltpu.make_async_remote_copy(
            src_ref=x_ref.at[peer],
            dst_ref=x_all.at[z, me],
            send_sem=x_send.at[peer],
            recv_sem=x_recv.at[me],
            device_id=(z, peer),
            device_id_type=MESH,
        )

    def x_arrival(peer):
        return pltpu.make_async_remote_copy(
            src_ref=x_ref.at[peer],
            dst_ref=x_all.at[z, peer],
            send_sem=x_send.at[peer],
            recv_sem=x_recv.at[peer],
            device_id=(z, peer),
            device_id_type=MESH,
        )

    def exchange(step, carry):
        x_copy(lax.rem(me + step, groups)).start()
        return carry

    lax.fori_loop(1, groups, exchange, 0)

    def line_copy(block, part, to, send_sem):
        if part == 0:
            view = g_all.at[block]
        else:
            view = x_all.at[block, pl.ds((part - 1) * per_part, per_part)]
        return pltpu.make_async_remote_copy(
            src_ref=view,
            dst_ref=view,
            send_sem=send_sem.at[block, part],
            recv_sem=line_recv.at[block, part],
            device_id=(to, me),
            device_id_type=MESH,
        )

    def to_right(block, part):
        return line_copy(block, part, z + 1, right_send)

    def to_left(block, part):
        return line_copy(block, part, z - 1, left_send)

    own_g.wait()
    row_index = lax.broadcasted_iota(jnp.int32, g_raw.shape, 0)
    live = row_index < BLK * counts_ref[0, me]
    g_all[z] = jnp.where(live, g_raw[...], jnp.zeros((), g_raw.dtype))

    for part in range(parts + 1):
        if part > 0:
            for peer in range((part - 1) * per_part, part * per_part):

                @pl.when(me == peer)
                def _():
                    own_x.wait()

                @pl.when(me != peer)
                def _():
                    x_arrival(peer).wait_recv()

        @pl.when(right_exists)
        def _():
            to_right(z, part).start()

        @pl.when(left_exists)
        def _():
            to_left(z, part).start()

    for step in range(1, replicas):
        for part in range(parts + 1):

            @pl.when(z >= step)
            def _():
                to_right(z - step, part).wait_recv()

                @pl.when(right_exists)
                def _():
                    to_right(z - step, part).start()

            @pl.when(z + step <= last)
            def _():
                to_left(z + step, part).wait_recv()

                @pl.when(left_exists)
                def _():
                    to_left(z + step, part).start()

    hidden = g_raw.shape[1]
    width = x_ref.shape[2]
    rows = replicas * capacity

    def gradient(group, total):
        block = contract_rows(
            x_all[:, group].reshape(rows, width), g_all[...].reshape(rows, hidden)
        )
        grad[group] = block.astype(jnp.bfloat16)
        return total + jnp.sum((block * block).reshape(width // 8, 8, hidden), axis=0)

    total = lax.fori_loop(0, groups, gradient, jnp.zeros((8, hidden), jnp.float32))
    norm = jnp.sqrt(jnp.sum(total, keepdims=True)) + EPSILON
    scale = 1.0 / norm
    gram_into(gram, grad, scale * scale)
    for iteration in range(ITERS - 1):
        source = grad if iteration == 0 else current
        polynomial_into(poly, gram)

        def advance(group, carry):
            combined = turn(source[group], poly)
            if iteration == 0:
                combined = combined * scale
            current[group] = combined.astype(jnp.bfloat16)
            return carry

        lax.fori_loop(0, groups, advance, 0)
        gram_into(gram, current, None)
    polynomial_into(poly, gram)

    def out_copy(peer):
        return pltpu.make_async_remote_copy(
            src_ref=stage.at[peer],
            dst_ref=out_ref.at[me],
            send_sem=out_send.at[peer],
            recv_sem=out_recv.at[me],
            device_id=(z, peer),
            device_id_type=MESH,
        )

    def out_arrival(peer):
        return pltpu.make_async_remote_copy(
            src_ref=stage.at[peer],
            dst_ref=out_ref.at[peer],
            send_sem=out_send.at[peer],
            recv_sem=out_recv.at[peer],
            device_id=(z, peer),
            device_id_type=MESH,
        )

    def finish(peer):
        stage[peer] = (turn(current[peer], poly) * math.sqrt(D)).astype(jnp.bfloat16)

    def send_out(step, carry):
        peer = lax.rem(me + step, groups)
        finish(peer)
        out_copy(peer).start()
        return carry

    lax.fori_loop(1, groups, send_out, 0)
    finish(me)
    own_out = pltpu.make_async_copy(stage.at[me], out_ref.at[me], local_sem.at[0])
    own_out.start()

    def settle(step, carry):
        peer = lax.rem(me + step, groups)
        x_copy(peer).wait_send()
        out_copy(peer).wait_send()
        out_arrival(peer).wait_recv()
        return carry

    lax.fori_loop(1, groups, settle, 0)
    own_out.wait()
    for step in range(replicas):
        for part in range(parts + 1):

            @pl.when(jnp.logical_and(z >= step, right_exists))
            def _():
                to_right(z - step, part).wait_send()

            @pl.when(jnp.logical_and(z + step <= last, left_exists))
            def _():
                to_left(z + step, part).wait_send()


def per_device(x_routed, grad_out, block_counts):
    groups = lax.axis_size("expert")
    replicas = lax.axis_size("dp")
    experts, capacity, width = x_routed.shape
    hidden = grad_out.shape[2]
    parts = 4
    dma = pltpu.SemaphoreType.DMA
    return pl.pallas_call(
        functools.partial(kernel, groups, replicas, parts),
        out_shape=jax.ShapeDtypeStruct((groups, width, hidden), jnp.bfloat16),
        in_specs=[
            pl.BlockSpec(memory_space=pltpu.SMEM),
            pl.BlockSpec(memory_space=pl.ANY),
            pl.BlockSpec(memory_space=pl.ANY),
        ],
        out_specs=pl.BlockSpec(memory_space=pl.ANY),
        scratch_shapes=[
            pltpu.VMEM((replicas, groups, capacity, width), jnp.bfloat16),
            pltpu.VMEM((replicas, capacity, hidden), jnp.bfloat16),
            pltpu.VMEM((capacity, hidden), jnp.bfloat16),
            pltpu.VMEM((groups, width, hidden), jnp.bfloat16),
            pltpu.VMEM((groups, width, hidden), jnp.bfloat16),
            pltpu.VMEM((groups, width, hidden), jnp.bfloat16),
            pltpu.VMEM((hidden, hidden), jnp.bfloat16),
            pltpu.VMEM((hidden, hidden), jnp.bfloat16),
            dma((2,)),
            dma((groups,)),
            dma((groups,)),
            dma((replicas, parts + 1)),
            dma((replicas, parts + 1)),
            dma((replicas, parts + 1)),
            dma((groups,)),
            dma((groups,)),
        ],
        compiler_params=pltpu.CompilerParams(
            collective_id=0, has_side_effects=True, vmem_limit_bytes=56 * 2**20
        ),
    )(block_counts, x_routed, grad_out)


def solution(mesh):
    return jax.shard_map(
        per_device,
        mesh=mesh,
        in_specs=(P(None, "dp", "expert"), P(None, "dp", None), P("dp", None)),
        out_specs=P(None, "expert", None),
        check_vma=False,
    )
```

time: 170 us -> 110 us (0.65); the launches traced: 168 us -> 110 us
  Pallas kernels: 0 us -> 106 us
  blocking collectives: 78.8 us -> 0 us
  matrix products: 39.7 us -> 0 us
  waiting for transfers between devices: 26.6 us -> 0 us
  between operations: 14.1 us -> 0.01 us
  other arithmetic: 2.91 us -> 0 us
  local copies, waits for them, and re-layouts: 6.15 us -> 3.76 us
    pallas_call x0 -> x1, Pallas kernels: none -> 106 us  [per_device(): pl.pallas_call(functools.partial(kernel, groups, replicas, parts), out_sh...]
    all_to_all x2 -> x0, blocking collectives: 53 us -> none  [the longest x1 39.5 us: per_device(): lax.all_to_all(arranged, 'expert', split_axis=0, concat_axis=0, tiled=True)]
    dot_general x5 -> x0, matrix products: 39.7 us -> none  [the longest x2 21 us: newton_turn(): jnp.dot(current, polynomial, preferred_element_type=jnp.float32)]
    all_gather x1 -> x0, waiting for transfers between devices: 26.5 us -> none  [per_device(): x_all = lax.all_gather(x_rows, 'dp', axis=0, tiled=True)]
    all_gather x1 -> x0, blocking collectives: 25.8 us -> none  [per_device(): g_all = lax.all_gather(g_rows, 'dp', axis=0, tiled=True)]
    reshape x1 -> x0, local copies, waits for them, and re-layouts: 3.18 us -> none  [per_device(): arranged = current.reshape(groups, slice_width, hidden_width)]
    unnamed x2 -> x1, local copies, waits for them, and re-layouts: 2.98 us -> 3.76 us
  transfers between devices with their start and end apart: 1 -> 0, of which waited for: 1 -> 0; matrix products, arithmetic and copies ran while one was open for 2% -> 0% of each run, Pallas kernels for 0% -> 0%
where the time goes in v2:
time: 110 us
  Pallas kernels  106 us (96%)
  local copies, waits for them, and re-layouts  3.76 us (3%)
    pallas_call x1, Pallas kernels, per_device(): pl.pallas_call(functools.partial(kernel, groups, replicas, parts), out_sh...  106 us
    unnamed x1, local copies, waits for them, and re-layouts  3.76 us

profile of v2, /device:TPU:1, one launch (start us, length us, event | category | flops | bytes accessed | tf_op | source)
XLA Modules:
  0.0 110.2 jit_solution(5994749396263728650)
XLA Ops:
  0.0 106.5 %shard_map.37 = bf16[8,256,768]{2,1,0:T(8,128)(2,1)} custom-call(s32[1,8]{1,0:T(1,128)} %counts_ref.1, bf16[8,128,256]{2,1,0:T(8,128)(2,1)} %x_ref.1, bf16[8,128,768]{2,1,0:T(8,128)(2,1)} %g_ref.1), custom_call_target="tpu_custom_call" | custom-call | tf_op jit(solution)/shard_map/pallas_call | solution.py:300
  106.5 3.8 %copy.5 = bf16[8,256,768]{2,1,0:T(8,128)(2,1)} copy(bf16[8,256,768]{2,1,0:T(8,128)(2,1)} %shard_map.37) | data formatting | bytes 6291456

commit v3 on v2

--- a/solution.py
+++ b/solution.py
@@ -81,6 +81,7 @@
     line_recv,
     out_send,
     out_recv,
+    handed,
 ):
     z = lax.axis_index("dp")
     me = lax.axis_index("expert")
@@ -141,11 +142,14 @@
 
     lax.fori_loop(1, groups, exchange, 0)
 
+    def chunk(part):
+        return lax.rem(me // per_part + part - 1, parts)
+
     def line_copy(block, part, to, send_sem):
         if part == 0:
             view = g_all.at[block]
         else:
-            view = x_all.at[block, pl.ds((part - 1) * per_part, per_part)]
+            view = x_all.at[block, pl.ds(chunk(part) * per_part, per_part)]
         return pltpu.make_async_remote_copy(
             src_ref=view,
             dst_ref=view,
@@ -166,25 +170,78 @@
     live = row_index < BLK * counts_ref[0, me]
     g_all[z] = jnp.where(live, g_raw[...], jnp.zeros((), g_raw.dtype))
 
-    for part in range(parts + 1):
-        if part > 0:
-            for peer in range((part - 1) * per_part, part * per_part):
-
-                @pl.when(me == peer)
-                def _():
-                    own_x.wait()
-
-                @pl.when(me != peer)
-                def _():
-                    x_arrival(peer).wait_recv()
-
-        @pl.when(right_exists)
-        def _():
-            to_right(z, part).start()
-
-        @pl.when(left_exists)
-        def _():
-            to_left(z, part).start()
+    even = lax.rem(me, 2) == 0
+    odd = jnp.logical_not(even)
+    low_half = 2 * z < replicas
+
+    def take_link(direction, exists):
+        @pl.when(jnp.logical_and(odd, exists))
+        def _():
+            pl.semaphore_wait(handed.at[direction], 1)
+
+    def give_link(direction, exists):
+        @pl.when(jnp.logical_and(even, exists))
+        def _():
+            pl.semaphore_signal(
+                handed.at[direction], inc=1, device_id=(z, me + 1), device_id_type=MESH
+            )
+
+    def start_right():
+        take_link(0, right_exists)
+        for part in range(parts + 1):
+
+            @pl.when(right_exists)
+            def _():
+                to_right(z, part).start()
+
+    def start_left():
+        take_link(1, left_exists)
+        for part in range(parts + 1):
+
+            @pl.when(left_exists)
+            def _():
+                to_left(z, part).start()
+
+    def own_chunk(part):
+        for offset in range(per_part):
+            peer = chunk(part) * per_part + offset
+
+            @pl.when(me == peer)
+            def _():
+                own_x.wait()
+
+            @pl.when(me != peer)
+            def _():
+                x_arrival(peer).wait_recv()
+
+    @pl.when(even)
+    def _():
+        for part in range(parts + 1):
+            if part > 0:
+                own_chunk(part)
+
+            @pl.when(right_exists)
+            def _():
+                to_right(z, part).start()
+
+            @pl.when(left_exists)
+            def _():
+                to_left(z, part).start()
+
+    @pl.when(odd)
+    def _():
+        for part in range(1, parts + 1):
+            own_chunk(part)
+
+        @pl.when(low_half)
+        def _():
+            start_right()
+            start_left()
+
+        @pl.when(jnp.logical_not(low_half))
+        def _():
+            start_left()
+            start_right()
 
     for step in range(1, replicas):
         for part in range(parts + 1):
@@ -204,6 +261,38 @@
                 @pl.when(left_exists)
                 def _():
                     to_left(z + step, part).start()
+
+    def sent_right(step, part):
+        @pl.when(jnp.logical_and(z >= step, right_exists))
+        def _():
+            to_right(z - step, part).wait_send()
+
+    def sent_left(step, part):
+        @pl.when(jnp.logical_and(z + step <= last, left_exists))
+        def _():
+            to_left(z + step, part).wait_send()
+
+    def release_right():
+        for step in range(replicas):
+            for part in range(parts):
+                sent_right(step, part)
+        give_link(0, right_exists)
+
+    def release_left():
+        for step in range(replicas):
+            for part in range(parts):
+                sent_left(step, part)
+        give_link(1, left_exists)
+
+    @pl.when(jnp.logical_and(even, low_half))
+    def _():
+        release_right()
+        release_left()
+
+    @pl.when(jnp.logical_and(even, jnp.logical_not(low_half)))
+    def _():
+        release_left()
+        release_right()
 
     hidden = g_raw.shape[1]
     width = x_ref.shape[2]
@@ -278,16 +367,17 @@
 
     lax.fori_loop(1, groups, settle, 0)
     own_out.wait()
+
+    @pl.when(odd)
+    def _():
+        for step in range(replicas):
+            for part in range(parts):
+                sent_right(step, part)
+                sent_left(step, part)
+
     for step in range(replicas):
-        for part in range(parts + 1):
-
-            @pl.when(jnp.logical_and(z >= step, right_exists))
-            def _():
-                to_right(z - step, part).wait_send()
-
-            @pl.when(jnp.logical_and(z + step <= last, left_exists))
-            def _():
-                to_left(z + step, part).wait_send()
+        sent_right(step, parts)
+        sent_left(step, parts)
 
 
 def per_device(x_routed, grad_out, block_counts):
@@ -323,6 +413,7 @@
             dma((replicas, parts + 1)),
             dma((groups,)),
             dma((groups,)),
+            pltpu.SemaphoreType.REGULAR((2,)),
         ],
         compiler_params=pltpu.CompilerParams(
             collective_id=0, has_side_effects=True, vmem_limit_bytes=56 * 2**20

time: 110 us -> 94.5 us (0.86)
  Pallas kernels: 106 us -> 90.6 us
    pallas_call x1, Pallas kernels: 106 us -> 90.6 us  [per_device(): pl.pallas_call(functools.partial(kernel, groups, replicas, parts), out_sh...]
where the time goes in v3:
time: 94.5 us; the launch traced here: 94.4 us
  Pallas kernels  90.6 us (96%)
  local copies, waits for them, and re-layouts  3.76 us (4%)
    pallas_call x1, Pallas kernels, per_device(): pl.pallas_call(functools.partial(kernel, groups, replicas, parts), out_sh...  90.6 us
    unnamed x1, local copies, waits for them, and re-layouts  3.76 us

profile of v3, /device:TPU:1, one launch (start us, length us, event | category | flops | bytes accessed | tf_op | source)
XLA Modules:
  0.0 94.4 jit_solution(8308108271035866002)
XLA Ops:
  0.0 90.6 %shard_map.37 = bf16[8,256,768]{2,1,0:T(8,128)(2,1)} custom-call(s32[1,8]{1,0:T(1,128)} %counts_ref.1, bf16[8,128,256]{2,1,0:T(8,128)(2,1)} %x_ref.1, bf16[8,128,768]{2,1,0:T(8,128)(2,1)} %g_ref.1), custom_call_target="tpu_custom_call" | custom-call | tf_op jit(solution)/shard_map/pallas_call | solution.py:390
  90.6 3.8 %copy.5 = bf16[8,256,768]{2,1,0:T(8,128)(2,1)} copy(bf16[8,256,768]{2,1,0:T(8,128)(2,1)} %shard_map.37) | data formatting | bytes 6291456

commit v4 on v3

--- a/solution.py
+++ b/solution.py
@@ -82,6 +82,7 @@
     out_send,
     out_recv,
     handed,
+    relay_send,
 ):
     z = lax.axis_index("dp")
     me = lax.axis_index("expert")
@@ -347,25 +348,94 @@
     def finish(peer):
         stage[peer] = (turn(current[peer], poly) * math.sqrt(D)).astype(jnp.bfloat16)
 
+    mirror = groups - 2 - 2 * (me // 2)
+    at_end = jnp.logical_or(z == 0, z == last)
+    relayed = mirror + 1
+    own_out = pltpu.make_async_copy(stage.at[me], out_ref.at[me], local_sem.at[0])
+
+    def sends(step):
+        if replicas < 3:
+            return step >= 0
+        skipped = jnp.logical_and(jnp.logical_and(odd, at_end), step < 2)
+        return jnp.logical_not(skipped)
+
     def send_out(step, carry):
-        peer = lax.rem(me + step, groups)
-        finish(peer)
-        out_copy(peer).start()
+        peer = lax.rem(mirror + step, groups)
+
+        @pl.when(sends(step))
+        def _():
+            finish(peer)
+
+            @pl.when(peer != me)
+            def _():
+                out_copy(peer).start()
+
+            @pl.when(peer == me)
+            def _():
+                own_out.start()
+
         return carry
 
-    lax.fori_loop(1, groups, send_out, 0)
-    finish(me)
-    own_out = pltpu.make_async_copy(stage.at[me], out_ref.at[me], local_sem.at[0])
-    own_out.start()
+    lax.fori_loop(0, groups, send_out, 0)
+
+    def relay(to):
+        return pltpu.make_async_remote_copy(
+            src_ref=out_ref.at[relayed],
+            dst_ref=out_ref.at[relayed],
+            send_sem=relay_send.at[to],
+            recv_sem=out_recv.at[relayed],
+            device_id=(to * last, me),
+            device_id_type=MESH,
+        )
+
+    if replicas >= 3:
+        inner = jnp.logical_or(z == 1, z == last - 1)
+
+        @pl.when(inner)
+        def _():
+            out_arrival(relayed).wait_recv()
+
+        @pl.when(z == 1)
+        def _():
+            relay(0).start()
+
+        @pl.when(z == last - 1)
+        def _():
+            relay(1).start()
 
     def settle(step, carry):
-        peer = lax.rem(me + step, groups)
-        x_copy(peer).wait_send()
-        out_copy(peer).wait_send()
-        out_arrival(peer).wait_recv()
+        peer = lax.rem(mirror + step, groups)
+
+        @pl.when(peer != me)
+        def _():
+            x_copy(peer).wait_send()
+
+            @pl.when(sends(step))
+            def _():
+                out_copy(peer).wait_send()
+
+            if replicas >= 3:
+
+                @pl.when(jnp.logical_not(jnp.logical_and(inner, peer == relayed)))
+                def _():
+                    out_arrival(peer).wait_recv()
+
+            else:
+                out_arrival(peer).wait_recv()
+
         return carry
 
-    lax.fori_loop(1, groups, settle, 0)
+    lax.fori_loop(0, groups, settle, 0)
+    if replicas >= 3:
+
+        @pl.when(z == 1)
+        def _():
+            relay(0).wait_send()
+
+        @pl.when(z == last - 1)
+        def _():
+            relay(1).wait_send()
+
     own_out.wait()
 
     @pl.when(odd)
@@ -414,6 +484,7 @@
             dma((groups,)),
             dma((groups,)),
             pltpu.SemaphoreType.REGULAR((2,)),
+            dma((2,)),
         ],
         compiler_params=pltpu.CompilerParams(
             collective_id=0, has_side_effects=True, vmem_limit_bytes=56 * 2**20

time: 94.5 us -> 87.4 us (0.925)
  Pallas kernels: 90.6 us -> 83.5 us
    pallas_call x1, Pallas kernels: 90.6 us -> 83.5 us  [per_device(): pl.pallas_call(functools.partial(kernel, groups, replicas, parts), out_sh...]
where the time goes in v4:
time: 87.4 us; the launch traced here: 87.3 us
  Pallas kernels  83.5 us (96%)
  local copies, waits for them, and re-layouts  3.76 us (4%)
    pallas_call x1, Pallas kernels, per_device(): pl.pallas_call(functools.partial(kernel, groups, replicas, parts), out_sh...  83.5 us
    unnamed x1, local copies, waits for them, and re-layouts  3.76 us

profile of v4, /device:TPU:1, one launch (start us, length us, event | category | flops | bytes accessed | tf_op | source)
XLA Modules:
  0.0 87.3 jit_solution(9800838095489288231)
XLA Ops:
  0.0 83.5 %shard_map.37 = bf16[8,256,768]{2,1,0:T(8,128)(2,1)} custom-call(s32[1,8]{1,0:T(1,128)} %counts_ref.1, bf16[8,128,256]{2,1,0:T(8,128)(2,1)} %x_ref.1, bf16[8,128,768]{2,1,0:T(8,128)(2,1)} %g_ref.1), custom_call_target="tpu_custom_call" | custom-call | tf_op jit(solution)/shard_map/pallas_call | solution.py:460
  83.5 3.8 %copy.5 = bf16[8,256,768]{2,1,0:T(8,128)(2,1)} copy(bf16[8,256,768]{2,1,0:T(8,128)(2,1)} %shard_map.37) | data formatting | bytes 6291456

commit v5 on v4

--- a/solution.py
+++ b/solution.py
@@ -459,13 +459,13 @@
     dma = pltpu.SemaphoreType.DMA
     return pl.pallas_call(
         functools.partial(kernel, groups, replicas, parts),
-        out_shape=jax.ShapeDtypeStruct((groups, width, hidden), jnp.bfloat16),
+        out_shape=pltpu.VMEM((groups, width, hidden), jnp.bfloat16),
         in_specs=[
             pl.BlockSpec(memory_space=pltpu.SMEM),
             pl.BlockSpec(memory_space=pl.ANY),
             pl.BlockSpec(memory_space=pl.ANY),
         ],
-        out_specs=pl.BlockSpec(memory_space=pl.ANY),
+        out_specs=pl.BlockSpec(memory_space=pltpu.VMEM),
         scratch_shapes=[
             pltpu.VMEM((replicas, groups, capacity, width), jnp.bfloat16),
             pltpu.VMEM((replicas, capacity, hidden), jnp.bfloat16),
@@ -487,7 +487,7 @@
             dma((2,)),
         ],
         compiler_params=pltpu.CompilerParams(
-            collective_id=0, has_side_effects=True, vmem_limit_bytes=56 * 2**20
+            collective_id=0, has_side_effects=True, vmem_limit_bytes=57 * 2**20
         ),
     )(block_counts, x_routed, grad_out)
 

time: 87.4 us -> 85.3 us (0.976)
  local copies, waits for them, and re-layouts: 3.76 us -> 1.67 us
    unnamed x1, local copies, waits for them, and re-layouts: 3.76 us -> 1.67 us
where the time goes in v5:
time: 85.3 us; the launch traced here: 85.2 us
  Pallas kernels  83.5 us (98%)
  local copies, waits for them, and re-layouts  1.67 us (2%)
    pallas_call x1, Pallas kernels, per_device(): pl.pallas_call(functools.partial(kernel, groups, replicas, parts), out_sh...  83.5 us

profile of v5, /device:TPU:1, one launch (start us, length us, event | category | flops | bytes accessed | tf_op | source)
XLA Modules:
  0.0 85.2 jit_solution(5943645649368191966)
XLA Ops:
  0.0 83.5 %shard_map.37 = bf16[8,256,768]{2,1,0:T(8,128)(2,1)S(1)} custom-call(s32[1,8]{1,0:T(1,128)} %counts_ref.1, bf16[8,128,256]{2,1,0:T(8,128)(2,1)} %x_ref.1, bf16[8,128,768]{2,1,0:T(8,128)(2,1)} %g_ref.1), custom_call_target="tpu_custom_call" | custom-call | tf_op jit(solution)/shard_map/pallas_call | solution.py:460
  83.5 1.7 %copy.5 = bf16[8,256,768]{2,1,0:T(8,128)(2,1)} copy(bf16[8,256,768]{2,1,0:T(8,128)(2,1)S(1)} %shard_map.37) | data formatting | bytes 6291456
